TPU v7x, 128 devices: a whole 4x4x4 slice. The times are simulated.
128 devices in a mesh: dp: 8 (over x, y_hi), tensor: 16 (over z, y_lo, core).
Axes of the slice: x: 4, y: 4 (y_hi: 2, y_lo: 2; y = y_hi * 2 + y_lo), z: 4, core: 2. Of those that a mesh axis runs over, the one named last changes fastest.
Arguments:
- grad_out: bfloat16 [2048, 9216], P(('dp', 'tensor')), may hold values from -0.3984375 to 0.3984375
- pre: bfloat16 [2048, 36864], P('dp', 'tensor'), may hold values from -6 to 6
- codes: int32 [36864, 9216], P('tensor', 'dp'), may hold values from 0 to 15
- exponents: int32 [288, 9216], P('tensor', 'dp'), may hold values from -7 to -4
Outputs:
- grad_pre: bfloat16 [2048, 36864], P('dp', 'tensor')
- grad_weight: float32 [36864, 9216], P('tensor', 'dp')
- grad_exponent: float32 [288, 9216], P('tensor', 'dp')
All inputs are finite; a program needn't handle non-finite values.
Results may differ from a plain program's by a relative error of at most 0.0028.
Values may be sent and summed in bfloat16 or wider, within the bound.
A program may use at most 128 MiB of HBM per device.

v0:
```python
import functools

import jax
import jax.numpy as jnp
from jax import lax
from jax.experimental import pallas as pl
from jax.experimental.pallas import tpu as pltpu
from jax.sharding import PartitionSpec as P

MESH = pl.DeviceIdType.MESH
LOG_TWO = 0.6931471805599453
NT = (((1,), (1,)), ((), ()))
BF16, F32, I16 = jnp.bfloat16, jnp.float32, jnp.int16

FF = 2304
WIDTH = 1152
ROWS = 256
HALF = ROWS // 2
GROUP = 128
LANES = 128
FX = 1280
FY = FF - FX
PIECES = (512, 384, 256, 128)
AX = 896
AY1 = 768
AY2 = FF - AX - AY1
TOP = 32700.0
UNIT = TOP * TOP
CHUNK = 256
N_GW = FF // CHUNK
SLOTS = 3


def encode(value):
    root = value * lax.rsqrt(jnp.maximum(jnp.abs(value), 1e-20))
    return jnp.round(root).astype(I16)


def decode(code):
    root = code.astype(jnp.int32).astype(F32)
    return root * jnp.abs(root)


def add_into(target, others, step=16):
    def some(i, carry):
        rows = pl.ds(pl.multiple_of(i * step, step), step)
        total = decode(target[rows, :])
        for other in others:
            total = total + decode(other[rows, :])
        target[rows, :] = encode(total)
        return carry

    lax.fori_loop(0, target.shape[0] // step, some, 0)


def kernel(
    go_hbm, pre_hbm, codes_ref, exp_hbm, gp_ref, gw_ref, ge_ref,
    go_ref, pre_ref, exp_ref, act, pq, g, w, gsrc, cbuf,
    x1a, x1b, xm, xp, xc, y1, ya, yb, ym, yp,
    ssem, rsem, csem, isem,
):
    j = lax.axis_index("dp")
    t = lax.axis_index("tensor")
    x, yh = j // 2, j % 2
    other = 1 - yh
    z, yl, core = t // 4, (t // 2) % 2, t % 2

    def blk(dx, hi):
        return ((x + dx) % 4) * 2 + hi

    def ten(dz):
        return ((z + dz) % 4) * 4 + yl * 2 + core

    east, west = (blk(1, yh), t), (blk(3, yh), t)
    across = (blk(0, other), t)
    up, down = (j, ten(1)), (j, ten(3))
    beside = (j, z * 4 + (1 - yl) * 2 + core)
    twin = (j, z * 4 + yl * 2 + 1 - core)
    peers = [((j + k) % 8, t) for k in range(1, 8)]

    barrier = pltpu.get_barrier_semaphore()
    for device in (*peers, up, down, beside, twin):
        pl.semaphore_signal(barrier, inc=1, device_id=device, device_id_type=MESH)

    copies = {}

    def send(name, src, dst, device):
        n = len(copies)
        copy = pltpu.make_async_remote_copy(
            src_ref=src, dst_ref=dst, send_sem=ssem.at[n], recv_sem=rsem.at[n],
            device_id=device, device_id_type=MESH,
        )
        copy.start()
        copies[name] = copy

    def same(name, view, device):
        send(name, view, view, device)

    def arrive(*names):
        for name in names:
            copies[name].wait_recv()

    spans = [pl.ds(AX, AY1), pl.ds(0, AX), pl.ds(AX + AY1, AY2)]
    pieces = []
    for n, span in enumerate(spans):
        pieces.append(pltpu.make_async_copy(pre_hbm.at[:, span], pre_ref.at[:, span], isem.at[n]))
    rows_load = pltpu.make_async_copy(go_hbm, go_ref, isem.at[3])
    exponents_load = pltpu.make_async_copy(exp_hbm, exp_ref, isem.at[4])
    for load in (pieces[0], rows_load, pieces[1], pieces[2], exponents_load):
        load.start()

    def fetch(i):
        slot = lax.rem(i, SLOTS)
        rows = pl.ds(pl.multiple_of(i * CHUNK, CHUNK), CHUNK)
        return pltpu.make_async_copy(codes_ref.at[rows, :], cbuf.at[slot], csem.at[slot])

    for i in range(SLOTS):
        fetch(i).start()

    def transpose(i, carry):
        columns = pl.ds(pl.multiple_of(i * LANES, LANES), LANES)
        positive = jnp.maximum(pre_ref[:, columns].astype(F32), 0.0)
        act[j, columns, :] = (positive * positive).astype(BF16).T
        return carry

    def piece(first, size):
        def rows(b, part=None):
            if part is None:
                return act.at[b, pl.ds(first, size), :]
            return act.at[b, pl.ds(first + part * (size // 2), size // 2), :]

        return rows

    y1_rows, x_rows, y2_rows = piece(AX, AY1), piece(0, AX), piece(AX + AY1, AY2)

    pieces[0].wait()
    lax.fori_loop(AX // LANES, (AX + AY1) // LANES, transpose, 0)

    rows_load.wait()
    total = jnp.zeros((16, 1), F32)
    for d in range(8):
        block = go_ref[:, d * WIDTH : (d + 1) * WIDTH]
        total = total + jnp.sum(jnp.abs(block.astype(F32)), axis=1, keepdims=True)
        gsrc[d, :, :WIDTH] = block
    scale = jnp.maximum(total * 0.51, 1e-36).astype(BF16)
    for d in range(8):
        gsrc[d, :, WIDTH:] = jnp.broadcast_to(scale, (16, LANES))
    mine = pl.ds(pl.multiple_of(t * 16, 16), 16)
    g[j, mine, :] = gsrc[j]

    pl.semaphore_wait(barrier, 11)

    for k in range(1, 8):
        d = (j + k) % 8
        send(f"a2a{k}", gsrc.at[d], g.at[j, mine, :], (d, t))
    same("ay1", y1_rows(j), across)
    same("ay1+", y1_rows(j), east)
    same("ay1-", y1_rows(j), west)
    pieces[1].wait()
    lax.fori_loop(0, AX // LANES, transpose, 0)
    same("ax+", x_rows(j), east)
    same("ax-", x_rows(j), west)
    pieces[2].wait()
    lax.fori_loop((AX + AY1) // LANES, FF // LANES, transpose, 0)
    exponents_load.wait()

    def dequantize(i, carry):
        fetch(i).wait()
        slot = lax.rem(i, SLOTS)
        for half in range(CHUNK // GROUP):
            exponent = exp_ref[pl.ds(i * (CHUNK // GROUP) + half, 1), :]
            power = jnp.zeros(exponent.shape, F32)
            for p in range(-7, -3):
                power = jnp.where(exponent == p, 2.0**p, power)
            code = cbuf[slot, half * GROUP : (half + 1) * GROUP, :]
            rows = pl.ds(pl.multiple_of(i * CHUNK + half * GROUP, GROUP), GROUP)
            w[rows, :] = ((code - 8).astype(F32) * power).astype(BF16)

        @pl.when(i + SLOTS < N_GW)
        def _():
            fetch(i + SLOTS).start()

        return carry

    lax.fori_loop(0, N_GW, dequantize, 0)

    def tokens(dz, hi, part=None):
        rows = pl.ds(pl.multiple_of((((z + dz) % 4) * 4 + hi * 2 + core) * 16, 16), 16)
        if part is None:
            return g.at[:, rows, :]
        return g.at[pl.ds(part * 4, 4), rows, :]

    arrive(*(f"a2a{k}" for k in range(1, 8)))
    same("gl", tokens(0, yl), beside)
    same("g+", tokens(0, yl), up)
    same("g-", tokens(0, yl), down)
    same("gc0", tokens(0, yl), twin)
    same("ay2", y2_rows(j), across)
    same("axy", x_rows(j), across)

    arrive("ay1")
    same("ayp1+", y1_rows(blk(0, other)), east)
    same("ayp1-", y1_rows(blk(0, other)), west)
    same("ay2+", y2_rows(j), east)
    same("ay2-", y2_rows(j), west)
    arrive("g+")
    same("gf+", tokens(3, yl, 0), up)
    same("gc2", tokens(3, yl), twin)
    arrive("g-")
    same("gf-", tokens(1, yl, 1), down)
    same("gc3", tokens(1, yl), twin)
    arrive("ay1+")
    same("ayf1+", y1_rows(blk(3, yh), 0), east)
    arrive("ay1-")
    same("ayf1-", y1_rows(blk(1, yh), 1), west)

    arrive("gl")
    same("gl+", tokens(0, 1 - yl), up)
    same("gl-", tokens(0, 1 - yl), down)
    same("gc1", tokens(0, 1 - yl), twin)

    def products(dz):
        zz = (z + dz) % 4
        rows = pl.ds(pl.multiple_of(zz * 64, 64), 64)
        size = 768

        def some(n, carry):
            columns = pl.ds(pl.multiple_of(n * size, size), size)
            part = lax.dot_general(
                g[:, rows, pl.ds(0, WIDTH)].reshape(512, WIDTH), w[columns, :], NT, preferred_element_type=F32
            )
            inverse = UNIT / g[:, rows, pl.ds(WIDTH, LANES)].astype(F32).reshape(512, LANES)
            part = part * jnp.concatenate([inverse] * (size // LANES), axis=1)
            pq[:, rows, columns] = encode(part).reshape(8, 64, size)
            return carry

        lax.fori_loop(0, FF // size, some, 0)

    arrive("gc0", "gc1")
    products(0)

    arrive("ax+")
    same("axf+", x_rows(blk(3, yh), 0), east)
    same("axy1", x_rows(blk(3, yh)), across)
    arrive("ax-")
    same("axf-", x_rows(blk(1, yh), 1), west)
    same("axy2", x_rows(blk(1, yh)), across)

    arrive("gl+")
    same("glf+", tokens(3, 1 - yl, 0), up)
    same("gc4", tokens(3, 1 - yl), twin)
    arrive("gl-")
    same("glf-", tokens(1, 1 - yl, 1), down)
    same("gc5", tokens(1, 1 - yl), twin)
    arrive("ay2")
    same("ayp2+", y2_rows(blk(0, other)), east)
    same("ayp2-", y2_rows(blk(0, other)), west)

    arrive("gc2", "gc4")
    products(3)
    arrive("gf+", "gf-", "glf+", "glf-")
    same("gc6", tokens(2, yl), twin)
    same("gc7", tokens(2, 1 - yl), twin)
    arrive("ay2+")
    same("ayf2+", y2_rows(blk(3, yh), 0), east)
    arrive("ay2-")
    same("ayf2-", y2_rows(blk(1, yh), 1), west)
    arrive("ayp1+")
    same("aypf1+", y1_rows(blk(3, other), 0), east)
    arrive("ayp1-")
    same("aypf1-", y1_rows(blk(1, other), 1), west)
    arrive("gc3", "gc5")
    products(1)
    arrive("gc6", "gc7")
    products(2)
    arrive("axf+")
    same("axy3", x_rows(blk(2, yh), 0), across)
    arrive("axf-")
    same("axy4", x_rows(blk(2, yh), 1), across)

    low, high, whole = pl.ds(0, HALF), pl.ds(HALF, HALF), pl.ds(0, ROWS)
    cx, cy = pl.ds(0, FX), pl.ds(FX, FY)

    def first(e):
        hi = other if e else yh
        send(f"h1+{e}", pq.at[blk(2, hi), low, cx], x1a.at[e], east)
        send(f"h1-{e}", pq.at[blk(2, hi), high, cx], x1b.at[e], west)

    def second(e):
        hi = other if e else yh
        send(f"h2+{e}", pq.at[blk(1, hi), high, cx], xm.at[e, high, :], east)
        send(f"h2-{e}", pq.at[blk(3, hi), low, cx], xp.at[e, low, :], west)

    first(1)
    for k in (2, 1, 3, 0):
        send(f"s{k}", pq.at[blk(k, other), whole, cy], y1.at[k], across)
    arrive("ayp2+")
    same("aypf2+", y2_rows(blk(3, other), 0), east)
    arrive("ayp2-")
    same("aypf2-", y2_rows(blk(1, other), 1), west)
    first(0)
    second(1)

    def relay(e):
        hi = other if e else yh
        arrive(f"h1+{e}")
        add_into(pq.at[blk(1, hi), low, cx], [x1a.at[e]])
        send(f"h3+{e}", pq.at[blk(1, hi), low, cx], xm.at[e, low, :], east)
        arrive(f"h1-{e}")
        add_into(pq.at[blk(3, hi), high, cx], [x1b.at[e]])
        send(f"h3-{e}", pq.at[blk(3, hi), high, cx], xp.at[e, high, :], west)

    relay(1)
    arrive("s2")
    add_into(pq.at[blk(2, yh), whole, cy], [y1.at[2]])
    send("t1+", pq.at[blk(2, yh), low, cy], ya, east)
    send("t1-", pq.at[blk(2, yh), high, cy], yb, west)
    second(0)
    relay(0)

    def weight_tiles(first):
        def some(slot, carry):
            i = first + slot
            rows = pl.ds(pl.multiple_of(i * CHUNK, CHUNK), CHUNK)
            left = jnp.concatenate([act[b, rows, :] for b in range(8)], axis=1)
            right = g[:, :, pl.ds(0, WIDTH)].reshape(8 * ROWS, WIDTH)
            tile = jnp.dot(left, right, preferred_element_type=F32)
            gw_ref[rows, :] = tile
            product = tile * w[rows, :].astype(F32)
            ge_ref[i] = LOG_TWO * jnp.sum(product.reshape(CHUNK // GROUP, GROUP, WIDTH), axis=1)
            return carry

        lax.fori_loop(0, SLOTS, some, 0)

    arrive("axy", "axy1", "axy2", "axy3", "axy4")
    arrive(*(f"{name}{n}{way}" for name in ("ayf", "aypf") for n in "12" for way in "+-"))
    weight_tiles(0)
    weight_tiles(SLOTS)

    arrive("s1")
    add_into(pq.at[blk(1, yh), high, cy], [y1.at[1, high, :]])
    send("t2+", pq.at[blk(1, yh), high, cy], ym.at[high, :], east)

    arrive("h2+1", "h2-1", "h3+1", "h3-1")
    spans, first_column = [], 0
    for size in PIECES:
        spans.append(pl.ds(first_column, size))
        first_column += size
    for n, part in enumerate(spans):
        add_into(pq.at[blk(0, other), whole, part], [xm.at[1, :, part], xp.at[1, :, part]])
        send(f"c{n}", pq.at[blk(0, other), whole, part], xc.at[:, part], across)

    arrive("s3")
    add_into(pq.at[blk(3, yh), low, cy], [y1.at[3, low, :]])
    send("t2-", pq.at[blk(3, yh), low, cy], yp.at[low, :], west)
    arrive("t1+")
    add_into(pq.at[blk(1, yh), low, cy], [y1.at[1, low, :], ya])
    send("t3+", pq.at[blk(1, yh), low, cy], ym.at[low, :], east)
    arrive("t1-")
    add_into(pq.at[blk(3, yh), high, cy], [y1.at[3, high, :], yb])
    send("t3-", pq.at[blk(3, yh), high, cy], yp.at[high, :], west)

    weight_tiles(2 * SLOTS)

    def finish(columns, parts):
        step = 16

        def some(i, carry):
            rows = pl.ds(pl.multiple_of(i * step, step), step)
            total = decode(pq[j, rows, columns])
            for part in parts:
                total = total + decode(part[rows, :])
            unit = g[j, rows, pl.ds(WIDTH, LANES)].astype(F32) * (2.0 / UNIT)
            positive = jnp.maximum(pre_ref[rows, columns].astype(F32), 0.0)
            unit = jnp.concatenate([unit] * (columns.size // LANES), axis=1)
            gp_ref[rows, columns] = (total * unit * positive).astype(BF16)
            return carry

        lax.fori_loop(0, ROWS // step, some, 0)

    def finish_x(n):
        arrive(f"c{n}")
        finish(spans[n], [r.at[:, spans[n]] for r in (xm.at[0], xp.at[0], xc)])

    arrive("h2+0", "h2-0", "h3+0", "h3-0")
    for n in range(len(PIECES) - 2):
        finish_x(n)
    arrive("s0", "t2+", "t2-", "t3+", "t3-")
    finish(cy, [y1.at[0], ym, yp])
    for n in range(len(PIECES) - 2, len(PIECES)):
        finish_x(n)

    for copy in copies.values():
        copy.wait_send()


def place(gp, gw, ge, gp_out, gw_out, ge_out, rows, sem):
    copies = []
    for i in range(N_GW):
        part = pl.ds(i * CHUNK, CHUNK)
        copies.append(pltpu.make_async_copy(gw.at[part, :], gw_out.at[part, :], sem.at[i]))
    copies.append(pltpu.make_async_copy(gp, gp_out, sem.at[N_GW]))
    for copy in copies:
        copy.start()
    per = CHUNK // GROUP
    for i in range(N_GW):
        rows[i * per : (i + 1) * per, :] = ge[i]
    last = pltpu.make_async_copy(rows, ge_out, sem.at[N_GW + 1])
    last.start()
    for copy in (*copies, last):
        copy.wait()


def body(grad_out, pre, codes, exponents):
    vmem, hbm = pl.BlockSpec(memory_space=pltpu.VMEM), pl.BlockSpec(memory_space=pl.ANY)
    n_copies = 80
    grad_pre, grad_weight, grad_exponent = pl.pallas_call(
        kernel,
        out_shape=(
            pltpu.VMEM((ROWS, FF), BF16),
            pltpu.VMEM((FF, WIDTH), F32),
            pltpu.VMEM((N_GW, CHUNK // GROUP, WIDTH), F32),
        ),
        in_specs=[pl.BlockSpec(memory_space=pltpu.HBM)] * 4,
        out_specs=(vmem, vmem, vmem),
        scratch_shapes=[
            pltpu.VMEM((16, 8 * WIDTH), BF16),
            pltpu.VMEM((ROWS, FF), BF16),
            pltpu.VMEM(exponents.shape, jnp.int32),
            pltpu.VMEM((8, FF, ROWS), BF16),
            pltpu.VMEM((8, ROWS, FF), I16),
            pltpu.VMEM((8, ROWS, WIDTH + LANES), BF16),
            pltpu.VMEM((FF, WIDTH), BF16),
            pltpu.VMEM((8, 16, WIDTH + LANES), BF16),
            pltpu.VMEM((SLOTS, CHUNK, WIDTH), jnp.int32),
            pltpu.VMEM((2, HALF, FX), I16),
            pltpu.VMEM((2, HALF, FX), I16),
            pltpu.VMEM((2, ROWS, FX), I16),
            pltpu.VMEM((2, ROWS, FX), I16),
            pltpu.VMEM((ROWS, FX), I16),
            pltpu.VMEM((4, ROWS, FY), I16),
            pltpu.VMEM((HALF, FY), I16),
            pltpu.VMEM((HALF, FY), I16),
            pltpu.VMEM((ROWS, FY), I16),
            pltpu.VMEM((ROWS, FY), I16),
            pltpu.SemaphoreType.DMA((n_copies,)),
            pltpu.SemaphoreType.DMA((n_copies,)),
            pltpu.SemaphoreType.DMA((SLOTS,)),
            pltpu.SemaphoreType.DMA((5,)),
        ],
        compiler_params=pltpu.CompilerParams(
            collective_id=0, has_side_effects=True, vmem_limit_bytes=46 * 2**20
        ),
        name="backward",
    )(grad_out, pre, codes, exponents)
    return pl.pallas_call(
        place,
        out_shape=(
            jax.ShapeDtypeStruct((ROWS, FF), BF16),
            jax.ShapeDtypeStruct((FF, WIDTH), F32),
            jax.ShapeDtypeStruct(exponents.shape, F32),
        ),
        in_specs=[vmem] * 3,
        out_specs=(hbm, hbm, hbm),
        scratch_shapes=[
            pltpu.VMEM(exponents.shape, F32),
            pltpu.SemaphoreType.DMA((N_GW + 2,)),
        ],
        compiler_params=pltpu.CompilerParams(vmem_limit_bytes=4 * 2**20),
        name="place",
    )(grad_pre, grad_weight, grad_exponent)


def solution(mesh):
    return jax.shard_map(
        body,
        mesh=mesh,
        in_specs=(
            P(("dp", "tensor"), None),
            P("dp", "tensor"),
            P("tensor", "dp"),
            P("tensor", "dp"),
        ),
        out_specs=(P("dp", "tensor"), P("tensor", "dp"), P("tensor", "dp")),
        check_vma=False,
    )
```

profile of v0, /device:TPU:0, one launch (start us, length us, event | category | flops | bytes accessed | tf_op | source)
XLA Modules:
  0.0 139.3 jit_solution(15099349184820461721)
XLA Ops:
  0.6 134.2 %backward.1 = (bf16[256,2304]{1,0:T(8,128)(2,1)S(1)}, f32[2304,1152]{1,0:T(8,128)S(1)}, f32[9,2,1152]{2,1,0:T(2,128)S(1)}) custom-call(bf16[16,9216]{1,0:T(8,128)(2,1)} %go_hbm.1, bf16[256,2304]{1,0:T(8,128)(2,1)} %pre_hbm.1, s32[2304,1152]{1,0:T(8,128)} %codes_ref.1, s32[18,1152]{1,0:T(8,128)} %exp_hbm.1), custom_call_target="tpu_custom_call" | custom-call | tf_op jit(solution)/shard_map/backward/pallas_call | solution.py:417
  134.9 4.4 %place.1 = (bf16[256,2304]{1,0:T(8,128)(2,1)}, f32[2304,1152]{1,0:T(8,128)}, f32[18,1152]{1,0:T(8,128)}) custom-call(bf16[256,2304]{1,0:T(8,128)(2,1)S(1)} %get-tuple-element.6.gp, f32[2304,1152]{1,0:T(8,128)S(1)} %get-tuple-element.7.gw, f32[9,2,1152]{2,1,0:T(2,128)S(1)} %get-tuple-element.8.ge), custom_call_target="tpu_custom_call" | custom-call | tf_op jit(solution)/shard_map/place/pallas_call | solution.py:456
where the time goes:
time: 139 us
  Pallas kernels  139 us (100%)
    pallas_call x1, Pallas kernels, body(): pl.pallas_call(kernel, out_shape=(pltpu.VMEM((ROWS, FF), BF16), pltpu.VME...  134 us
    pallas_call x1, Pallas kernels, body(): pl.pallas_call(place, out_shape=(jax.ShapeDtypeStruct((ROWS, FF), BF16),...  4.44 us

commit v1 on v0

--- a/solution.py
+++ b/solution.py
@@ -23,6 +23,7 @@
 PIECES = (512, 384, 256, 128)
 AX = 896
 AY1 = 768
+EARLY = 256
 AY2 = FF - AX - AY1
 TOP = 32700.0
 UNIT = TOP * TOP
@@ -41,7 +42,16 @@
     return root * jnp.abs(root)
 
 
-def add_into(target, others, step=16):
+def step_of(rows, columns):
+    step = 16
+    while step * 2 <= rows and step * 2 * columns <= 16 * 2048:
+        step *= 2
+    return step
+
+
+def add_into(target, others):
+    step = step_of(*target.shape)
+
     def some(i, carry):
         rows = pl.ds(pl.multiple_of(i * step, step), step)
         total = decode(target[rows, :])
@@ -100,13 +110,13 @@
         for name in names:
             copies[name].wait_recv()
 
-    spans = [pl.ds(AX, AY1), pl.ds(0, AX), pl.ds(AX + AY1, AY2)]
+    spans = [pl.ds(AX, EARLY), pl.ds(AX + EARLY, AY1 - EARLY), pl.ds(0, AX), pl.ds(AX + AY1, AY2)]
     pieces = []
     for n, span in enumerate(spans):
         pieces.append(pltpu.make_async_copy(pre_hbm.at[:, span], pre_ref.at[:, span], isem.at[n]))
-    rows_load = pltpu.make_async_copy(go_hbm, go_ref, isem.at[3])
+    rows_load = pltpu.make_async_copy(go_hbm, go_ref, isem.at[5])
     exponents_load = pltpu.make_async_copy(exp_hbm, exp_ref, isem.at[4])
-    for load in (pieces[0], rows_load, pieces[1], pieces[2], exponents_load):
+    for load in (pieces[0], rows_load, *pieces[1:], exponents_load):
         load.start()
 
     def fetch(i):
@@ -134,7 +144,16 @@
     y1_rows, x_rows, y2_rows = piece(AX, AY1), piece(0, AX), piece(AX + AY1, AY2)
 
     pieces[0].wait()
-    lax.fori_loop(AX // LANES, (AX + AY1) // LANES, transpose, 0)
+    lax.fori_loop(AX // LANES, (AX + EARLY) // LANES, transpose, 0)
+
+    def early(name, start, end):
+        view = act.at[j, pl.ds(AX + start, end - start), :]
+        same(name, view, across)
+        same(f"{name}+", view, east)
+        same(f"{name}-", view, west)
+
+    pl.semaphore_wait(barrier, 11)
+    early("ay0", 0, EARLY)
 
     rows_load.wait()
     total = jnp.zeros((16, 1), F32)
@@ -148,19 +167,18 @@
     mine = pl.ds(pl.multiple_of(t * 16, 16), 16)
     g[j, mine, :] = gsrc[j]
 
-    pl.semaphore_wait(barrier, 11)
 
     for k in range(1, 8):
         d = (j + k) % 8
         send(f"a2a{k}", gsrc.at[d], g.at[j, mine, :], (d, t))
-    same("ay1", y1_rows(j), across)
-    same("ay1+", y1_rows(j), east)
-    same("ay1-", y1_rows(j), west)
     pieces[1].wait()
+    lax.fori_loop((AX + EARLY) // LANES, (AX + AY1) // LANES, transpose, 0)
+    early("ay1", EARLY, AY1)
+    pieces[2].wait()
     lax.fori_loop(0, AX // LANES, transpose, 0)
     same("ax+", x_rows(j), east)
     same("ax-", x_rows(j), west)
-    pieces[2].wait()
+    pieces[3].wait()
     lax.fori_loop((AX + AY1) // LANES, FF // LANES, transpose, 0)
     exponents_load.wait()
 
@@ -198,7 +216,7 @@
     same("ay2", y2_rows(j), across)
     same("axy", x_rows(j), across)
 
-    arrive("ay1")
+    arrive("ay0", "ay1")
     same("ayp1+", y1_rows(blk(0, other)), east)
     same("ayp1-", y1_rows(blk(0, other)), west)
     same("ay2+", y2_rows(j), east)
@@ -209,9 +227,9 @@
     arrive("g-")
     same("gf-", tokens(1, yl, 1), down)
     same("gc3", tokens(1, yl), twin)
-    arrive("ay1+")
+    arrive("ay0+", "ay1+")
     same("ayf1+", y1_rows(blk(3, yh), 0), east)
-    arrive("ay1-")
+    arrive("ay0-", "ay1-")
     same("ayf1-", y1_rows(blk(1, yh), 1), west)
 
     arrive("gl")
@@ -363,7 +381,7 @@
     weight_tiles(2 * SLOTS)
 
     def finish(columns, parts):
-        step = 16
+        step = step_of(ROWS, columns.size)
 
         def some(i, carry):
             rows = pl.ds(pl.multiple_of(i * step, step), step)
@@ -382,6 +400,10 @@
         arrive(f"c{n}")
         finish(spans[n], [r.at[:, spans[n]] for r in (xm.at[0], xp.at[0], xc)])
 
+    late = {"s0", "t2+", "t2-", "t3+", "t3-", *(f"c{n}" for n in range(len(PIECES)))}
+    for name in copies:
+        if name not in late:
+            copies[name].wait_send()
     arrive("h2+0", "h2-0", "h3+0", "h3-0")
     for n in range(len(PIECES) - 2):
         finish_x(n)
@@ -390,8 +412,9 @@
     for n in range(len(PIECES) - 2, len(PIECES)):
         finish_x(n)
 
-    for copy in copies.values():
-        copy.wait_send()
+    for name in copies:
+        if name in late:
+            copies[name].wait_send()
 
 
 def place(gp, gw, ge, gp_out, gw_out, ge_out, rows, sem):
@@ -446,7 +469,7 @@
             pltpu.SemaphoreType.DMA((n_copies,)),
             pltpu.SemaphoreType.DMA((n_copies,)),
             pltpu.SemaphoreType.DMA((SLOTS,)),
-            pltpu.SemaphoreType.DMA((5,)),
+            pltpu.SemaphoreType.DMA((6,)),
         ],
         compiler_params=pltpu.CompilerParams(
             collective_id=0, has_side_effects=True, vmem_limit_bytes=46 * 2**20

time: 139 us -> 139 us (level)
  no operation moved by 1% of the time
where the time goes in v1:
time: 139 us
  Pallas kernels  138 us (99%)
    pallas_call x1, Pallas kernels, body(): pl.pallas_call(kernel, out_shape=(pltpu.VMEM((ROWS, FF), BF16), pltpu.VME...  134 us
    pallas_call x1, Pallas kernels, body(): pl.pallas_call(place, out_shape=(jax.ShapeDtypeStruct((ROWS, FF), BF16),...  4.44 us

profile of v1, /device:TPU:0, one launch (start us, length us, event | category | flops | bytes accessed | tf_op | source)
XLA Modules:
  0.0 138.9 jit_solution(3126784099679958196)
XLA Ops:
  0.6 133.8 %backward.1 = (bf16[256,2304]{1,0:T(8,128)(2,1)S(1)}, f32[2304,1152]{1,0:T(8,128)S(1)}, f32[9,2,1152]{2,1,0:T(2,128)S(1)}) custom-call(bf16[16,9216]{1,0:T(8,128)(2,1)} %go_hbm.1, bf16[256,2304]{1,0:T(8,128)(2,1)} %pre_hbm.1, s32[2304,1152]{1,0:T(8,128)} %codes_ref.1, s32[18,1152]{1,0:T(8,128)} %exp_hbm.1), custom_call_target="tpu_custom_call" | custom-call | tf_op jit(solution)/shard_map/backward/pallas_call | solution.py:440
  134.5 4.4 %place.1 = (bf16[256,2304]{1,0:T(8,128)(2,1)}, f32[2304,1152]{1,0:T(8,128)}, f32[18,1152]{1,0:T(8,128)}) custom-call(bf16[256,2304]{1,0:T(8,128)(2,1)S(1)} %get-tuple-element.6.gp, f32[2304,1152]{1,0:T(8,128)S(1)} %get-tuple-element.7.gw, f32[9,2,1152]{2,1,0:T(2,128)S(1)} %get-tuple-element.8.ge), custom_call_target="tpu_custom_call" | custom-call | tf_op jit(solution)/shard_map/place/pallas_call | solution.py:479

commit v2 on v1

--- a/solution.py
+++ b/solution.py
@@ -20,7 +20,7 @@
 LANES = 128
 FX = 1280
 FY = FF - FX
-PIECES = (512, 384, 256, 128)
+PIECES = (112, 80, 48, 16)
 AX = 896
 AY1 = 768
 EARLY = 256
@@ -44,7 +44,7 @@
 
 def step_of(rows, columns):
     step = 16
-    while step * 2 <= rows and step * 2 * columns <= 16 * 2048:
+    while rows % (step * 2) == 0 and step * 2 * columns <= 16 * 2048:
         step *= 2
     return step
 
@@ -65,7 +65,7 @@
 
 def kernel(
     go_hbm, pre_hbm, codes_ref, exp_hbm, gp_ref, gw_ref, ge_ref,
-    go_ref, pre_ref, exp_ref, act, pq, g, w, gsrc, cbuf,
+    go_ref, pre_ref, exp_ref, act, pqx, pqy, g, w, gsrc, cbuf,
     x1a, x1b, xm, xp, xc, y1, ya, yb, ym, yp,
     ssem, rsem, csem, isem,
 ):
@@ -240,19 +240,24 @@
     def products(dz):
         zz = (z + dz) % 4
         rows = pl.ds(pl.multiple_of(zz * 64, 64), 64)
-        size = 768
-
-        def some(n, carry):
-            columns = pl.ds(pl.multiple_of(n * size, size), size)
-            part = lax.dot_general(
-                g[:, rows, pl.ds(0, WIDTH)].reshape(512, WIDTH), w[columns, :], NT, preferred_element_type=F32
-            )
-            inverse = UNIT / g[:, rows, pl.ds(WIDTH, LANES)].astype(F32).reshape(512, LANES)
-            part = part * jnp.concatenate([inverse] * (size // LANES), axis=1)
-            pq[:, rows, columns] = encode(part).reshape(8, 64, size)
-            return carry
-
-        lax.fori_loop(0, FF // size, some, 0)
+        left = g[:, rows, pl.ds(0, WIDTH)].reshape(512, WIDTH)
+        inverse = UNIT / g[:, rows, pl.ds(WIDTH, LANES)].astype(F32).reshape(512, LANES)
+
+        def fill(target, first):
+            size = target.shape[2] // 2
+
+            def some(n, carry):
+                units = pl.ds(pl.multiple_of(first + n * size, LANES), size)
+                columns = pl.ds(pl.multiple_of(n * size, LANES), size)
+                part = lax.dot_general(left, w[units, :], NT, preferred_element_type=F32)
+                part = part * jnp.concatenate([inverse] * (size // LANES), axis=1)
+                target[:, rows, columns] = encode(part).reshape(8, 64, size)
+                return carry
+
+            lax.fori_loop(0, 2, some, 0)
+
+        fill(pqx, 0)
+        fill(pqy, FX)
 
     arrive("gc0", "gc1")
     products(0)
@@ -297,21 +302,20 @@
     same("axy4", x_rows(blk(2, yh), 1), across)
 
     low, high, whole = pl.ds(0, HALF), pl.ds(HALF, HALF), pl.ds(0, ROWS)
-    cx, cy = pl.ds(0, FX), pl.ds(FX, FY)
 
     def first(e):
         hi = other if e else yh
-        send(f"h1+{e}", pq.at[blk(2, hi), low, cx], x1a.at[e], east)
-        send(f"h1-{e}", pq.at[blk(2, hi), high, cx], x1b.at[e], west)
+        send(f"h1+{e}", pqx.at[blk(2, hi), low], x1a.at[e], east)
+        send(f"h1-{e}", pqx.at[blk(2, hi), high], x1b.at[e], west)
 
     def second(e):
         hi = other if e else yh
-        send(f"h2+{e}", pq.at[blk(1, hi), high, cx], xm.at[e, high, :], east)
-        send(f"h2-{e}", pq.at[blk(3, hi), low, cx], xp.at[e, low, :], west)
+        send(f"h2+{e}", pqx.at[blk(1, hi), high], xm.at[e, high, :], east)
+        send(f"h2-{e}", pqx.at[blk(3, hi), low], xp.at[e, low, :], west)
 
     first(1)
     for k in (2, 1, 3, 0):
-        send(f"s{k}", pq.at[blk(k, other), whole, cy], y1.at[k], across)
+        send(f"s{k}", pqy.at[blk(k, other), whole], y1.at[k], across)
     arrive("ayp2+")
     same("aypf2+", y2_rows(blk(3, other), 0), east)
     arrive("ayp2-")
@@ -322,17 +326,17 @@
     def relay(e):
         hi = other if e else yh
         arrive(f"h1+{e}")
-        add_into(pq.at[blk(1, hi), low, cx], [x1a.at[e]])
-        send(f"h3+{e}", pq.at[blk(1, hi), low, cx], xm.at[e, low, :], east)
+        add_into(pqx.at[blk(1, hi), low], [x1a.at[e]])
+        send(f"h3+{e}", pqx.at[blk(1, hi), low], xm.at[e, low, :], east)
         arrive(f"h1-{e}")
-        add_into(pq.at[blk(3, hi), high, cx], [x1b.at[e]])
-        send(f"h3-{e}", pq.at[blk(3, hi), high, cx], xp.at[e, high, :], west)
+        add_into(pqx.at[blk(3, hi), high], [x1b.at[e]])
+        send(f"h3-{e}", pqx.at[blk(3, hi), high], xp.at[e, high, :], west)
 
     relay(1)
     arrive("s2")
-    add_into(pq.at[blk(2, yh), whole, cy], [y1.at[2]])
-    send("t1+", pq.at[blk(2, yh), low, cy], ya, east)
-    send("t1-", pq.at[blk(2, yh), high, cy], yb, west)
+    add_into(pqy.at[blk(2, yh), whole], [y1.at[2]])
+    send("t1+", pqy.at[blk(2, yh), low], ya, east)
+    send("t1-", pqy.at[blk(2, yh), high], yb, west)
     second(0)
     relay(0)
 
@@ -356,59 +360,58 @@
     weight_tiles(SLOTS)
 
     arrive("s1")
-    add_into(pq.at[blk(1, yh), high, cy], [y1.at[1, high, :]])
-    send("t2+", pq.at[blk(1, yh), high, cy], ym.at[high, :], east)
+    add_into(pqy.at[blk(1, yh), high], [y1.at[1, high, :]])
+    send("t2+", pqy.at[blk(1, yh), high], ym.at[high, :], east)
 
     arrive("h2+1", "h2-1", "h3+1", "h3-1")
-    spans, first_column = [], 0
-    for size in PIECES:
-        spans.append(pl.ds(first_column, size))
-        first_column += size
+    spans = [pl.ds(sum(PIECES[:n]), size) for n, size in enumerate(PIECES)]
     for n, part in enumerate(spans):
-        add_into(pq.at[blk(0, other), whole, part], [xm.at[1, :, part], xp.at[1, :, part]])
-        send(f"c{n}", pq.at[blk(0, other), whole, part], xc.at[:, part], across)
+        add_into(pqx.at[blk(0, other), part], [xm.at[1, part], xp.at[1, part]])
+        send(f"c{n}", pqx.at[blk(0, other), part], xc.at[part], across)
 
     arrive("s3")
-    add_into(pq.at[blk(3, yh), low, cy], [y1.at[3, low, :]])
-    send("t2-", pq.at[blk(3, yh), low, cy], yp.at[low, :], west)
+    add_into(pqy.at[blk(3, yh), low], [y1.at[3, low, :]])
+    send("t2-", pqy.at[blk(3, yh), low], yp.at[low, :], west)
     arrive("t1+")
-    add_into(pq.at[blk(1, yh), low, cy], [y1.at[1, low, :], ya])
-    send("t3+", pq.at[blk(1, yh), low, cy], ym.at[low, :], east)
+    add_into(pqy.at[blk(1, yh), low], [y1.at[1, low, :], ya])
+    send("t3+", pqy.at[blk(1, yh), low], ym.at[low, :], east)
     arrive("t1-")
-    add_into(pq.at[blk(3, yh), high, cy], [y1.at[3, high, :], yb])
-    send("t3-", pq.at[blk(3, yh), high, cy], yp.at[high, :], west)
+    add_into(pqy.at[blk(3, yh), high], [y1.at[3, high, :], yb])
+    send("t3-", pqy.at[blk(3, yh), high], yp.at[high, :], west)
 
     weight_tiles(2 * SLOTS)
 
-    def finish(columns, parts):
-        step = step_of(ROWS, columns.size)
+    def finish(own, span, first, parts):
+        size = own.shape[1]
+        step = step_of(span.size, size)
+        columns = pl.ds(first, size)
 
         def some(i, carry):
-            rows = pl.ds(pl.multiple_of(i * step, step), step)
-            total = decode(pq[j, rows, columns])
+            rows = pl.ds(pl.multiple_of(span.start + i * step, 16), step)
+            total = decode(own[rows, :])
             for part in parts:
                 total = total + decode(part[rows, :])
             unit = g[j, rows, pl.ds(WIDTH, LANES)].astype(F32) * (2.0 / UNIT)
             positive = jnp.maximum(pre_ref[rows, columns].astype(F32), 0.0)
-            unit = jnp.concatenate([unit] * (columns.size // LANES), axis=1)
+            unit = jnp.concatenate([unit] * (size // LANES), axis=1)
             gp_ref[rows, columns] = (total * unit * positive).astype(BF16)
             return carry
 
-        lax.fori_loop(0, ROWS // step, some, 0)
-
-    def finish_x(n):
-        arrive(f"c{n}")
-        finish(spans[n], [r.at[:, spans[n]] for r in (xm.at[0], xp.at[0], xc)])
+        lax.fori_loop(0, span.size // step, some, 0)
 
     late = {"s0", "t2+", "t2-", "t3+", "t3-", *(f"c{n}" for n in range(len(PIECES)))}
     for name in copies:
         if name not in late:
             copies[name].wait_send()
     arrive("h2+0", "h2-0", "h3+0", "h3-0")
+    def finish_x(n):
+        arrive(f"c{n}")
+        finish(pqx.at[j], spans[n], 0, [xm.at[0], xp.at[0], xc])
+
     for n in range(len(PIECES) - 2):
         finish_x(n)
     arrive("s0", "t2+", "t2-", "t3+", "t3-")
-    finish(cy, [y1.at[0], ym, yp])
+    finish(pqy.at[j], whole, FX, [y1.at[0], ym, yp])
     for n in range(len(PIECES) - 2, len(PIECES)):
         finish_x(n)
 
@@ -451,7 +454,8 @@
             pltpu.VMEM((ROWS, FF), BF16),
             pltpu.VMEM(exponents.shape, jnp.int32),
             pltpu.VMEM((8, FF, ROWS), BF16),
-            pltpu.VMEM((8, ROWS, FF), I16),
+            pltpu.VMEM((8, ROWS, FX), I16),
+            pltpu.VMEM((8, ROWS, FY), I16),
             pltpu.VMEM((8, ROWS, WIDTH + LANES), BF16),
             pltpu.VMEM((FF, WIDTH), BF16),
             pltpu.VMEM((8, 16, WIDTH + LANES), BF16),

time: 139 us -> 139 us (level)
  no operation moved by 1% of the time
where the time goes in v2:
time: 139 us
  Pallas kernels  138 us (99%)
    pallas_call x1, Pallas kernels, body(): pl.pallas_call(kernel, out_shape=(pltpu.VMEM((ROWS, FF), BF16), pltpu.VME...  134 us
    pallas_call x1, Pallas kernels, body(): pl.pallas_call(place, out_shape=(jax.ShapeDtypeStruct((ROWS, FF), BF16),...  4.44 us

profile of v2, /device:TPU:0, one launch (start us, length us, event | category | flops | bytes accessed | tf_op | source)
XLA Modules:
  0.0 138.9 jit_solution(2231605949258210906)
XLA Ops:
  0.6 133.8 %backward.1 = (bf16[256,2304]{1,0:T(8,128)(2,1)S(1)}, f32[2304,1152]{1,0:T(8,128)S(1)}, f32[9,2,1152]{2,1,0:T(2,128)S(1)}) custom-call(bf16[16,9216]{1,0:T(8,128)(2,1)} %go_hbm.1, bf16[256,2304]{1,0:T(8,128)(2,1)} %pre_hbm.1, s32[2304,1152]{1,0:T(8,128)} %codes_ref.1, s32[18,1152]{1,0:T(8,128)} %exp_hbm.1), custom_call_target="tpu_custom_call" | custom-call | tf_op jit(solution)/shard_map/backward/pallas_call | solution.py:443
  134.4 4.4 %place.1 = (bf16[256,2304]{1,0:T(8,128)(2,1)}, f32[2304,1152]{1,0:T(8,128)}, f32[18,1152]{1,0:T(8,128)}) custom-call(bf16[256,2304]{1,0:T(8,128)(2,1)S(1)} %get-tuple-element.6.gp, f32[2304,1152]{1,0:T(8,128)S(1)} %get-tuple-element.7.gw, f32[9,2,1152]{2,1,0:T(2,128)S(1)} %get-tuple-element.8.ge), custom_call_target="tpu_custom_call" | custom-call | tf_op jit(solution)/shard_map/place/pallas_call | solution.py:483

commit v3 on v2

--- a/solution.py
+++ b/solution.py
@@ -23,7 +23,7 @@
 PIECES = (112, 80, 48, 16)
 AX = 896
 AY1 = 768
-EARLY = 256
+EARLY = 128
 AY2 = FF - AX - AY1
 TOP = 32700.0
 UNIT = TOP * TOP

time: 139 us -> 139 us (level)
  no operation moved by 1% of the time
where the time goes in v3:
time: 139 us
  Pallas kernels  138 us (99%)
    pallas_call x1, Pallas kernels, body(): pl.pallas_call(kernel, out_shape=(pltpu.VMEM((ROWS, FF), BF16), pltpu.VME...  134 us
    pallas_call x1, Pallas kernels, body(): pl.pallas_call(place, out_shape=(jax.ShapeDtypeStruct((ROWS, FF), BF16),...  4.44 us

profile of v3, /device:TPU:0, one launch (start us, length us, event | category | flops | bytes accessed | tf_op | source)
XLA Modules:
  0.0 138.9 jit_solution(13933941206129388015)
XLA Ops:
  0.6 133.8 %backward.1 = (bf16[256,2304]{1,0:T(8,128)(2,1)S(1)}, f32[2304,1152]{1,0:T(8,128)S(1)}, f32[9,2,1152]{2,1,0:T(2,128)S(1)}) custom-call(bf16[16,9216]{1,0:T(8,128)(2,1)} %go_hbm.1, bf16[256,2304]{1,0:T(8,128)(2,1)} %pre_hbm.1, s32[2304,1152]{1,0:T(8,128)} %codes_ref.1, s32[18,1152]{1,0:T(8,128)} %exp_hbm.1), custom_call_target="tpu_custom_call" | custom-call | tf_op jit(solution)/shard_map/backward/pallas_call | solution.py:443
  134.4 4.4 %place.1 = (bf16[256,2304]{1,0:T(8,128)(2,1)}, f32[2304,1152]{1,0:T(8,128)}, f32[18,1152]{1,0:T(8,128)}) custom-call(bf16[256,2304]{1,0:T(8,128)(2,1)S(1)} %get-tuple-element.6.gp, f32[2304,1152]{1,0:T(8,128)S(1)} %get-tuple-element.7.gw, f32[9,2,1152]{2,1,0:T(2,128)S(1)} %get-tuple-element.8.ge), custom_call_target="tpu_custom_call" | custom-call | tf_op jit(solution)/shard_map/place/pallas_call | solution.py:483

commit v4 on v3

--- a/solution.py
+++ b/solution.py
@@ -88,10 +88,6 @@
     twin = (j, z * 4 + yl * 2 + 1 - core)
     peers = [((j + k) % 8, t) for k in range(1, 8)]
 
-    barrier = pltpu.get_barrier_semaphore()
-    for device in (*peers, up, down, beside, twin):
-        pl.semaphore_signal(barrier, inc=1, device_id=device, device_id_type=MESH)
-
     copies = {}
 
     def send(name, src, dst, device):
@@ -116,7 +112,13 @@
         pieces.append(pltpu.make_async_copy(pre_hbm.at[:, span], pre_ref.at[:, span], isem.at[n]))
     rows_load = pltpu.make_async_copy(go_hbm, go_ref, isem.at[5])
     exponents_load = pltpu.make_async_copy(exp_hbm, exp_ref, isem.at[4])
-    for load in (pieces[0], rows_load, *pieces[1:], exponents_load):
+    pieces[0].start()
+
+    barrier = pltpu.get_barrier_semaphore()
+    for device in (*peers, up, down, beside, twin):
+        pl.semaphore_signal(barrier, inc=1, device_id=device, device_id_type=MESH)
+
+    for load in (rows_load, *pieces[1:], exponents_load):
         load.start()
 
     def fetch(i):

time: 139 us -> 139 us (level)
  no operation moved by 1% of the time
where the time goes in v4:
time: 139 us
  Pallas kernels  138 us (99%)
    pallas_call x1, Pallas kernels, body(): pl.pallas_call(kernel, out_shape=(pltpu.VMEM((ROWS, FF), BF16), pltpu.VME...  134 us
    pallas_call x1, Pallas kernels, body(): pl.pallas_call(place, out_shape=(jax.ShapeDtypeStruct((ROWS, FF), BF16),...  4.44 us

profile of v4, /device:TPU:0, one launch (start us, length us, event | category | flops | bytes accessed | tf_op | source)
XLA Modules:
  0.0 138.9 jit_solution(1800818409546706938)
XLA Ops:
  0.6 133.8 %backward.1 = (bf16[256,2304]{1,0:T(8,128)(2,1)S(1)}, f32[2304,1152]{1,0:T(8,128)S(1)}, f32[9,2,1152]{2,1,0:T(2,128)S(1)}) custom-call(bf16[16,9216]{1,0:T(8,128)(2,1)} %go_hbm.1, bf16[256,2304]{1,0:T(8,128)(2,1)} %pre_hbm.1, s32[2304,1152]{1,0:T(8,128)} %codes_ref.1, s32[18,1152]{1,0:T(8,128)} %exp_hbm.1), custom_call_target="tpu_custom_call" | custom-call | tf_op jit(solution)/shard_map/backward/pallas_call | solution.py:445
  134.4 4.4 %place.1 = (bf16[256,2304]{1,0:T(8,128)(2,1)}, f32[2304,1152]{1,0:T(8,128)}, f32[18,1152]{1,0:T(8,128)}) custom-call(bf16[256,2304]{1,0:T(8,128)(2,1)S(1)} %get-tuple-element.6.gp, f32[2304,1152]{1,0:T(8,128)S(1)} %get-tuple-element.7.gw, f32[9,2,1152]{2,1,0:T(2,128)S(1)} %get-tuple-element.8.ge), custom_call_target="tpu_custom_call" | custom-call | tf_op jit(solution)/shard_map/place/pallas_call | solution.py:485
